TPU v7x, 32 devices: a whole 2x2x4 slice. The times are simulated.
32 devices in a mesh: section: 2 (over core), peer: 16 (over z, y, x).
Axes of the slice: x: 2, y: 2, z: 4, core: 2. Of those that a mesh axis runs over, the one named last changes fastest.
Arguments:
- arrivals: bfloat16 [2, 16, 64, 5120], P('section', 'peer'), may hold values from -6 to 6
- kept: bfloat16 [2, 16, 64, 5120], P('section', 'peer'), may hold values from -8 to 8
- returned: bfloat16 [2, 16, 64, 5120], P('section', 'peer'), may hold values from -8 to 8
- onward: int32 [2, 16], P('section'), may hold values from 0 to 15, each once within a row
- backward_route: int32 [2, 16], P('section'), may hold values from 0 to 15, each once within a row
- replicas: bfloat16 [2, 16, 5120, 128], P('section', 'peer'), may hold values from -6 to 6
- master: float32 [2, 5120, 128], P('section', 'peer'), may hold values from -0.6 to 0.6
- moment: float32 [2, 5120, 128], P('section', 'peer'), may hold values from -4 to 4
- second: float32 [2, 5120, 128], P('section', 'peer'), may hold values from 0.1 to 10
Outputs:
- handed_on: bfloat16 [2, 16, 64, 5120], P('section', 'peer')
- passed_back: bfloat16 [2, 16, 64, 5120], P('section', 'peer')
- new_master: float32 [2, 5120, 128], P('section', 'peer')
- new_moment: float32 [2, 5120, 128], P('section', 'peer')
- new_second: float32 [2, 5120, 128], P('section', 'peer')
Inputs may be any that keep to these rules, and one draw needn't show every extreme that they name: `onward`: each row lists every peer index once. `backward_route`: each row lists every peer index once.
All inputs are finite; a program needn't handle non-finite values.
Results may differ from a plain program's by a relative error of at most 0.004.
Values may be sent and summed in bfloat16 or wider, within the bound.
A program may use at most 64 MiB of HBM per device.

v0:
```python
import jax
import jax.numpy as jnp
from jax import lax
from jax.sharding import PartitionSpec as P

norm_eps = 1e-05
beta_first = 0.9
beta_second = 0.95
adam_eps = 1e-08
learn_rate = 0.05
weight_decay = 0.1
first_correction = 1.0 - 0.9**10
second_correction = 1.0 - 0.95**10


def shifted(block, axis, distance):
    devices = range(lax.axis_size(axis))
    route = [((i - distance) % len(devices), i) for i in devices]
    return lax.ppermute(block, axis, route)


def norm_rate(values):
    return lax.rsqrt(jnp.mean(values * values, axis=-1, keepdims=True) + norm_eps)


def inverse_order(targets):
    positions = jnp.arange(targets.shape[0], dtype=jnp.int32)
    matches = (targets[:, None] == positions[None, :]).astype(jnp.int32)
    return jnp.sum(matches * positions[:, None], axis=0)


def forward_layer(tokens, weights, inner_rank):
    features = tokens.shape[-1]
    values = tokens.astype(jnp.float32)
    normed = (values * norm_rate(values)).astype(jnp.bfloat16)
    hidden = jnp.dot(
        normed, weights[:, :inner_rank], preferred_element_type=jnp.float32
    ) * features ** (-0.5)
    active = jax.nn.silu(hidden).astype(jnp.bfloat16)
    branch = lax.dot_general(
        active,
        weights[:, inner_rank:],
        (((1,), (1,)), ((), ())),
        preferred_element_type=jnp.float32,
    )
    return (values + branch * inner_rank ** (-0.5)).astype(jnp.bfloat16)


def backward_layer(tokens, weights, upstream, inner_rank):
    features = tokens.shape[-1]
    values = tokens.astype(jnp.float32)
    scaling = norm_rate(values)
    normed = (values * scaling).astype(jnp.bfloat16)
    hidden = jnp.dot(
        normed, weights[:, :inner_rank], preferred_element_type=jnp.float32
    ) * features ** (-0.5)
    active = jax.nn.silu(hidden).astype(jnp.bfloat16)
    grad_active = jnp.dot(
        upstream, weights[:, inner_rank:], preferred_element_type=jnp.float32
    ) * inner_rank ** (-0.5)
    logistic = jax.nn.sigmoid(hidden)
    grad_hidden = (grad_active * logistic * (1.0 + hidden * (1.0 - logistic))).astype(jnp.bfloat16)
    grad_down = lax.dot_general(
        upstream, active, (((0,), (0,)), ((), ())), preferred_element_type=jnp.float32
    ) * inner_rank ** (-0.5)
    grad_up = lax.dot_general(
        normed, grad_hidden, (((0,), (0,)), ((), ())), preferred_element_type=jnp.float32
    ) * features ** (-0.5)
    grad_normed = lax.dot_general(
        grad_hidden,
        weights[:, :inner_rank],
        (((1,), (1,)), ((), ())),
        preferred_element_type=jnp.float32,
    ) * features ** (-0.5)
    mixed = jnp.mean(grad_normed * values, axis=-1, keepdims=True)
    grad_tokens = upstream.astype(jnp.float32) + scaling * grad_normed - values * scaling**3 * mixed
    return (grad_tokens.astype(jnp.bfloat16), jnp.concatenate([grad_up, grad_down], axis=1))


def spread_pair(onward_rows, backward_rows, onward_order, backward_order):
    sent_onward, sent_backward = (
        lax.all_to_all(onward_rows, "peer", split_axis=0, concat_axis=0, tiled=True),
        lax.all_to_all(backward_rows, "peer", split_axis=0, concat_axis=0, tiled=True),
    )
    return (
        jnp.take(sent_onward, onward_order, axis=0),
        jnp.take(sent_backward, backward_order, axis=0),
    )


def collect_pair(onward_middle, backward_middle):
    return (
        lax.all_to_all(onward_middle, "peer", split_axis=0, concat_axis=0, tiled=True),
        lax.all_to_all(backward_middle, "peer", split_axis=0, concat_axis=0, tiled=True),
    )


def hop_pair(onward_block, backward_block):
    forward_hop = shifted(onward_block, "section", 1)
    reverse_hop = shifted(backward_block, "section", -1)
    return (forward_hop, reverse_hop)


def shards(arrivals, kept, returned, onward, backward_route, replicas, master, moment, second):
    peer_count = lax.axis_size("peer")
    weights = replicas[0, 0]
    inner_rank = weights.shape[1] // 2
    tokens_in = arrivals[0, 0]
    token_count, features = tokens_in.shape
    piece_rows = token_count // peer_count
    produced = forward_layer(tokens_in, weights, inner_rank)
    grad_tokens, gradient = backward_layer(kept[0, 0], weights, returned[0, 0], inner_rank)
    onward_order = inverse_order(onward[0])
    backward_order = inverse_order(backward_route[0])
    onward_middle, backward_middle = spread_pair(
        produced.reshape(peer_count, piece_rows, features),
        grad_tokens.reshape(peer_count, piece_rows, features),
        onward_order,
        backward_order,
    )
    onward_done, backward_done = collect_pair(onward_middle, backward_middle)
    handed, passed = hop_pair(onward_done, backward_done)
    handed = handed.reshape(1, 1, token_count, features)
    passed = passed.reshape(1, 1, token_count, features)
    shard_rows = master.shape[1]
    summed = lax.psum(gradient, "peer")
    grad_rows = lax.dynamic_slice_in_dim(summed, lax.axis_index("peer") * shard_rows, shard_rows, 0)
    master_rows = master[0]
    new_moment = beta_first * moment[0] + (1.0 - beta_first) * grad_rows
    new_second = beta_second * second[0] + (1.0 - beta_second) * grad_rows * grad_rows
    update = new_moment / first_correction / (jnp.sqrt(new_second / second_correction) + adam_eps)
    new_master = master_rows - learn_rate * (update + weight_decay * master_rows)
    return (handed, passed, new_master[None], new_moment[None], new_second[None])


def solution(mesh):
    return jax.shard_map(
        shards,
        mesh=mesh,
        in_specs=(
            P("section", "peer", None, None),
            P("section", "peer", None, None),
            P("section", "peer", None, None),
            P("section", None),
            P("section", None),
            P("section", "peer", None, None),
            P("section", "peer", None),
            P("section", "peer", None),
            P("section", "peer", None),
        ),
        out_specs=(
            P("section", "peer", None, None),
            P("section", "peer", None, None),
            P("section", "peer", None),
            P("section", "peer", None),
            P("section", "peer", None),
        ),
        check_vma=False,
    )
```

profile of v0, /device:TPU:15, one launch (start us, length us, event | category | flops | bytes accessed | tf_op | source)
XLA Modules:
  0.0 198.1 jit_solution(9127996476624472021)
XLA Ops:
  7.2 1.3 fusion.5
  8.5 0.0 copy-start.1
  8.5 0.0 copy-start.2
  8.5 2.0 %convolution_multiply_fusion.3 = f32[64,64]{1,0:T(8,128)S(1)} fusion(bf16[5120,128]{1,0:T(8,128)(2,1)} %bitcast.62, bf16[1,1,64,5120]{3,2,1,0:T(8,128)(2,1)} %param.12, f32[64]{0:T(128)S(1)} %get-tuple-element.17), kind=kOutput, calls=%fused_computation.29 | convolution fusion | flops 42930176 | bytes 1982720 | tf_op jit(solution)/shard_map/dot_general | solution.py:54
  10.6 0.0 copy-done.1
  10.6 0.0 copy-done.2
  10.6 0.0 copy-start
  10.6 0.6 fusion.23
  11.2 0.5 copy-done
  11.7 0.7 fusion.10
  12.4 0.4 fusion.9
  12.8 1.1 reshape.65
  13.9 6.6 %all-to-all-start.2 = ((bf16[16,4,5120]{2,1,0:T(4,128)(2,1)}), bf16[16,4,5120]{2,1,0:T(4,128)(2,1)S(1)}, u32[]{:S(2)}, u32[]{:S(2)}) async-start(bf16[16,4,5120]{2,1,0:T(4,128)(2,1)} %reshape.65), calls=%async_computation.2 | async-start | bytes 1310720 | tf_op jit(solution)/shard_map/all_to_all | solution.py:83
  20.5 0.0 all-reduce.2.cloned.1.call-start
  20.5 0.4 convolution_multiply_fusion.1
  20.9 0.4 fusion.1
  21.3 1.7 pad_maximum_fusion
  23.0 0.0 copy-start.3
  23.0 0.0 all-reduce.2.cloned.1.call-update
  23.0 1.1 copy-done.3
  24.1 0.2 fusion.3
  24.3 1.0 fusion.2
  25.3 0.0 copy-start.7
  25.3 0.0 copy-start.8
  25.3 1.1 reshape.63
  26.4 0.0 copy-done.7
  26.4 0.1 select_reduce_fusion
  26.5 0.0 copy-done.8
  26.5 0.1 select_reduce_fusion.1
  26.6 9.2 %all-to-all-done.2 = bf16[16,4,5120]{2,1,0:T(4,128)(2,1)S(1)} async-done(((bf16[16,4,5120]{2,1,0:T(4,128)(2,1)}), bf16[16,4,5120]{2,1,0:T(4,128)(2,1)S(1)}, u32[]{:S(2)}, u32[]{:S(2)}) %all-to-all-start.2) | async-done | bytes 655392 | tf_op jit(solution)/shard_map/all_to_all | solution.py:83
  35.8 6.8 %all-to-all-start = ((bf16[16,4,5120]{2,1,0:T(4,128)(2,1)}), bf16[16,4,5120]{2,1,0:T(4,128)(2,1)S(1)}, u32[]{:S(2)}, u32[]{:S(2)}) async-start(bf16[16,4,5120]{2,1,0:T(4,128)(2,1)} %reshape.63), calls=%async_computation | async-start | bytes 1310720 | tf_op jit(solution)/shard_map/all_to_all | solution.py:82
  42.7 1.1 gather_fusion.1
  43.8 1.2 broadcast_select_fusion
  45.0 26.1 %all-to-all-done = bf16[16,4,5120]{2,1,0:T(4,128)(2,1)S(1)} async-done(((bf16[16,4,5120]{2,1,0:T(4,128)(2,1)}), bf16[16,4,5120]{2,1,0:T(4,128)(2,1)S(1)}, u32[]{:S(2)}, u32[]{:S(2)}) %all-to-all-start) | async-done | bytes 655392 | tf_op jit(solution)/shard_map/all_to_all | solution.py:82
  71.1 5.4 %all-to-all-start.3 = ((bf16[16,4,5120]{2,1,0:T(4,128)(2,1)}), bf16[16,4,5120]{2,1,0:T(4,128)(2,1)S(1)}, u32[]{:S(2)}, u32[]{:S(2)}) async-start(bf16[16,4,5120]{2,1,0:T(4,128)(2,1)} %broadcast_select_fusion), calls=%async_computation.3 | async-start | bytes 1310720 | tf_op jit(solution)/shard_map/all_to_all | solution.py:94
  76.5 1.1 gather_fusion
  77.7 0.0 copy-start.4
  77.7 0.0 copy-start.5
  77.7 1.2 broadcast_select_fusion.1
  78.9 0.0 copy-start.6
  78.9 18.8 %all-to-all-done.3 = bf16[16,4,5120]{2,1,0:T(4,128)(2,1)S(1)} async-done(((bf16[16,4,5120]{2,1,0:T(4,128)(2,1)}), bf16[16,4,5120]{2,1,0:T(4,128)(2,1)S(1)}, u32[]{:S(2)}, u32[]{:S(2)}) %all-to-all-start.3) | async-done | bytes 655392 | tf_op jit(solution)/shard_map/all_to_all | solution.py:94
  97.6 5.3 %all-to-all-start.1 = ((bf16[16,4,5120]{2,1,0:T(4,128)(2,1)}), bf16[16,4,5120]{2,1,0:T(4,128)(2,1)S(1)}, u32[]{:S(2)}, u32[]{:S(2)}) async-start(bf16[16,4,5120]{2,1,0:T(4,128)(2,1)} %broadcast_select_fusion.1), calls=%async_computation.1 | async-start | bytes 1310720 | tf_op jit(solution)/shard_map/all_to_all | solution.py:93
  103.0 1.9 collective-permute-start.1
  104.9 15.2 %all-to-all-done.1 = bf16[16,4,5120]{2,1,0:T(4,128)(2,1)S(1)} async-done(((bf16[16,4,5120]{2,1,0:T(4,128)(2,1)}), bf16[16,4,5120]{2,1,0:T(4,128)(2,1)S(1)}, u32[]{:S(2)}, u32[]{:S(2)}) %all-to-all-start.1) | async-done | bytes 655392 | tf_op jit(solution)/shard_map/all_to_all | solution.py:93
  120.1 1.7 collective-permute-start
  121.8 0.0 copy-done.4
  121.8 0.1 copy.20
  121.9 0.0 copy-done.5
  121.9 0.1 copy.21
  122.1 0.0 copy-done.6
  122.1 0.1 copy.22
  122.2 62.3 %all-reduce.2.cloned.1.call-done = f32[5120,128]{0,1:T(8,128)} async-done(((f32[5120,128]{0,1:T(8,128)}), f32[5120,128]{0,1:T(8,128)}) %all-reduce.2.cloned.1.call-update) | async-done | bytes 2621456 | tf_op jit(solution)/shard_map/psum | solution.py:126
  184.5 1.2 fusion.42
  185.7 0.8 copy.23
  186.4 0.8 copy.24
  187.2 0.8 copy.25
  188.0 0.0 collective-permute-done.1
  188.0 1.0 reshape.66
  189.0 0.0 collective-permute-done
  189.0 2.2 %reshape.64 = bf16[1,1,64,5120]{3,2,1,0:T(8,128)(2,1)} reshape(bf16[16,4,5120]{2,1,0:T(4,128)(2,1)} %collective-permute-done) | data formatting | bytes 1310720 | tf_op jit(solution)/shard_map/reshape | solution.py:123
  (10 shorter events, 0.1 us)
Async XLA Ops:
  8.5 2.1 %copy-start.1 = (bf16[1,1,64,5120]{3,2,1,0:T(8,128)(2,1)S(1)}, bf16[1,1,64,5120]{3,2,1,0:T(8,128)(2,1)}, u32[]{:S(2)}) copy-start(bf16[1,1,64,5120]{3,2,1,0:T(8,128)(2,1)} %param.13) | copy-start | bytes 1966084
  8.5 2.1 %copy-start.2 = (bf16[1,1,5120,128]{3,2,1,0:T(8,128)(2,1)S(1)}, bf16[1,1,5120,128]{3,2,1,0:T(8,128)(2,1)}, u32[]{:S(2)}) copy-start(bf16[1,1,5120,128]{3,2,1,0:T(8,128)(2,1)} %param.16) | copy-start | bytes 3932164
  10.6 1.1 copy-start
  13.9 21.9 %all-to-all-start.2 = ((bf16[16,4,5120]{2,1,0:T(4,128)(2,1)}), bf16[16,4,5120]{2,1,0:T(4,128)(2,1)S(1)}, u32[]{:S(2)}, u32[]{:S(2)}) async-start(bf16[16,4,5120]{2,1,0:T(4,128)(2,1)} %reshape.65), calls=%async_computation.2 | async-start | bytes 1310720 | tf_op jit(solution)/shard_map/all_to_all | solution.py:83
  20.5 164.0 %all-reduce.2.cloned.1.call-start = ((), (), s32[]{:S(2)}) async-start(), calls=%async_computation.4 | async-start | bytes 5242880 | tf_op jit(solution)/shard_map/psum | solution.py:126
  23.0 1.1 copy-start.3
  25.3 1.1 copy-start.7
  25.3 1.2 copy-start.8
  35.8 35.3 %all-to-all-start = ((bf16[16,4,5120]{2,1,0:T(4,128)(2,1)}), bf16[16,4,5120]{2,1,0:T(4,128)(2,1)S(1)}, u32[]{:S(2)}, u32[]{:S(2)}) async-start(bf16[16,4,5120]{2,1,0:T(4,128)(2,1)} %reshape.63), calls=%async_computation | async-start | bytes 1310720 | tf_op jit(solution)/shard_map/all_to_all | solution.py:82
  71.1 26.5 %all-to-all-start.3 = ((bf16[16,4,5120]{2,1,0:T(4,128)(2,1)}), bf16[16,4,5120]{2,1,0:T(4,128)(2,1)S(1)}, u32[]{:S(2)}, u32[]{:S(2)}) async-start(bf16[16,4,5120]{2,1,0:T(4,128)(2,1)} %broadcast_select_fusion), calls=%async_computation.3 | async-start | bytes 1310720 | tf_op jit(solution)/shard_map/all_to_all | solution.py:94
  77.7 44.2 %copy-start.4 = (f32[1,320,128]{2,1,0:T(8,128)S(1)}, f32[1,320,128]{2,1,0:T(8,128)}, u32[]{:S(2)}) copy-start(f32[1,320,128]{2,1,0:T(8,128)} %param.17) | copy-start | bytes 491524
  77.7 44.3 %copy-start.5 = (f32[1,320,128]{2,1,0:T(8,128)S(1)}, f32[1,320,128]{2,1,0:T(8,128)}, u32[]{:S(2)}) copy-start(f32[1,320,128]{2,1,0:T(8,128)} %param.18) | copy-start | bytes 491524
  78.9 43.2 %copy-start.6 = (f32[1,320,128]{2,1,0:T(8,128)S(1)}, f32[1,320,128]{2,1,0:T(8,128)}, u32[]{:S(2)}) copy-start(f32[1,320,128]{2,1,0:T(8,128)} %param.19) | copy-start | bytes 491524
  97.6 22.5 %all-to-all-start.1 = ((bf16[16,4,5120]{2,1,0:T(4,128)(2,1)}), bf16[16,4,5120]{2,1,0:T(4,128)(2,1)S(1)}, u32[]{:S(2)}, u32[]{:S(2)}) async-start(bf16[16,4,5120]{2,1,0:T(4,128)(2,1)} %broadcast_select_fusion.1), calls=%async_computation.1 | async-start | bytes 1310720 | tf_op jit(solution)/shard_map/all_to_all | solution.py:93
  103.0 85.0 %collective-permute-start.1 = (bf16[16,4,5120]{2,1,0:T(4,128)(2,1)S(1)}, bf16[16,4,5120]{2,1,0:T(4,128)(2,1)S(1)}, u32[]{:S(2)}, u32[]{:S(2)}) collective-permute-start(bf16[16,4,5120]{2,1,0:T(4,128)(2,1)S(1)} %all-to-all-done.3), channel_id=1, source_target_pairs={{16,0},{0,16},{17,1},{1,17},{18,2},{2,18},{19,3},{3,19},{20,4},{4,... | collective-permute-start | bytes 1966088 | tf_op jit(solution)/shard_map/ppermute | solution.py:19
  120.1 68.9 %collective-permute-start = (bf16[16,4,5120]{2,1,0:T(4,128)(2,1)S(1)}, bf16[16,4,5120]{2,1,0:T(4,128)(2,1)}, u32[]{:S(2)}, u32[]{:S(2)}) collective-permute-start(bf16[16,4,5120]{2,1,0:T(4,128)(2,1)S(1)} %all-to-all-done.1), channel_id=1, source_target_pairs={{16,0},{0,16},{17,1},{1,17},{18,2},{2,18},{19,3},{3,19},{20,4},{4,... | collective-permute-start | bytes 1966088 | tf_op jit(solution)/shard_map/ppermute | solution.py:19
Sparse Core Ops, SparseCore 0:
  26.9 157.5 all-reduce.1
where the time goes:
time: 201 us; the launch traced here: 198 us
  waiting for transfers between devices  132 us (66%)
  starting transfers between devices  27.8 us (14%)
  between operations  14.2 us (7%)
  local copies, waits for them, and re-layouts  11.9 us (6%)
  other arithmetic  7.48 us (4%)
  matrix products  5.05 us (3%)
    psum x1, waiting for transfers between devices, shards(): summed = lax.psum(gradient, 'peer')  62.3 us
    all_to_all x1, waiting for transfers between devices, spread_pair(): lax.all_to_all(onward_rows, 'peer', split_axis=0, concat_axis=0, tiled=True)  26.1 us
    all_to_all x1, waiting for transfers between devices, collect_pair(): lax.all_to_all(backward_middle, 'peer', split_axis=0, concat_axis=0, tile...  18.8 us
    all_to_all x1, waiting for transfers between devices, collect_pair(): lax.all_to_all(onward_middle, 'peer', split_axis=0, concat_axis=0, tiled=...  15.2 us
    all_to_all x1, waiting for transfers between devices, spread_pair(): lax.all_to_all(backward_rows, 'peer', split_axis=0, concat_axis=0, tiled=...  9.18 us
    all_to_all x1, starting transfers between devices, spread_pair(): lax.all_to_all(onward_rows, 'peer', split_axis=0, concat_axis=0, tiled=True)  6.83 us
    all_to_all x1, starting transfers between devices, spread_pair(): lax.all_to_all(backward_rows, 'peer', split_axis=0, concat_axis=0, tiled=...  6.58 us
    all_to_all x1, starting transfers between devices, collect_pair(): lax.all_to_all(backward_middle, 'peer', split_axis=0, concat_axis=0, tile...  5.42 us
  transfers between devices with their start and end apart: 7, of which 5 were waited for; matrix products, arithmetic and copies ran while one was open for 7% of the time, Pallas kernels for 0%

commit v1 on v0

v1 whole, which is shorter than its diff:
```python
import functools
import math

import jax
import jax.numpy as jnp
from jax import lax
from jax.experimental import pallas as pl
from jax.experimental.pallas import tpu as pltpu
from jax.sharding import PartitionSpec as P

norm_eps = 1e-05
beta_first = 0.9
beta_second = 0.95
adam_eps = 1e-08
learn_rate = 0.05
weight_decay = 0.1
first_correction = 1.0 - 0.9**10
second_correction = 1.0 - 0.95**10

ROWS = 16
MESH = pl.DeviceIdType.MESH
F32, BF16 = jnp.float32, jnp.bfloat16


def inverse_order(targets):
    positions = jnp.arange(targets.shape[0], dtype=jnp.int32)
    matches = (targets[:, None] == positions[None, :]).astype(jnp.int32)
    return jnp.sum(matches * positions[:, None], axis=0)


def column_chunks(width, parts):
    step = width // parts
    return [(i * step, step) for i in range(parts)]


def kernel(
    sections, peers, inner, width,
    source_on, source_back, arrivals, kept, returned, weights, master, moment, second,
    handed, passed, new_master, new_moment, new_second,
    made, landed_on, landed_back, outgoing, grad_normed, stacked, grad_wide, grad_sent, grad_landed,
    part_wide, part_sent, part_landed, sems,
):
    token_count, features = arrivals.shape
    rank = weights.shape[1] // 2
    outer = peers // inner
    col_groups = peers // (token_count // ROWS)
    shard = master.shape[0]
    sec, me = lax.axis_index("section"), lax.axis_index("peer")
    plane, spot = me // inner, lax.rem(me, inner)
    onto = lax.rem(sec + 1, sections)
    back = lax.rem(sec + sections - 1, sections)

    landings = (landed_on, landed_back)
    barrier = pltpu.get_barrier_semaphore()

    def greet(section, first):
        def one(k, carry):
            target = lax.rem(me + k, peers)
            pl.semaphore_signal(barrier, inc=1, device_id=(section, target), device_id_type=MESH)
            return carry
        lax.fori_loop(first, peers, one, 0)

    greet(sec, 1)
    greet(onto, 0)
    greeted = 2 * peers - 1
    if sections > 2:
        greet(back, 0)
        greeted += peers

    def piece(j):
        row = pl.multiple_of((j // col_groups) * ROWS, ROWS)
        col = pl.multiple_of(lax.rem(j, col_groups) * width, 128)
        return pl.ds(row, ROWS), pl.ds(col, width)

    def spread(t):
        def one(k, carry):
            j = lax.rem(me + k, peers)
            rows, cols = piece(j)
            pltpu.make_async_remote_copy(
                made.at[t, rows, cols], landings[t].at[me], sems.at[t], sems.at[2 + t],
                device_id=(sec, j), device_id_type=MESH,
            ).start()
            return carry
        lax.fori_loop(1, peers, one, 0)
        rows, cols = piece(me)
        pltpu.make_async_copy(made.at[t, rows, cols], landings[t].at[me], sems.at[2 + t]).start()

    def collect(t, order, section, result):
        pltpu.make_async_copy(landings[t], landings[t], sems.at[2 + t]).wait()
        rows, cols = piece(me)

        def one(k, carry):
            d = lax.rem(me + k, peers)
            outgoing[t, d] = landings[t][order[d]]
            pltpu.make_async_remote_copy(
                outgoing.at[t, d], result.at[rows, cols], sems.at[4 + t], sems.at[6 + t],
                device_id=(section, d), device_id_type=MESH,
            ).start()
            return carry
        lax.fori_loop(0, peers, one, 0)

    chunks = column_chunks(features, 4)
    if made.shape[2] > features:
        made[:, :, features:] = jnp.zeros((2, token_count, made.shape[2] - features), BF16)

    def rate(ref):
        total = jnp.zeros((token_count, 128), F32)
        for start, size in chunks:
            x = ref[:, start:start + size].astype(F32)
            x = x * x
            for c in range(0, size, 128):
                total += x[:, c:c + 128]
        return lax.rsqrt(jnp.sum(total, axis=1, keepdims=True) * (1.0 / features) + norm_eps)

    right = lax.broadcasted_iota(jnp.int32, (token_count, 2 * rank), 1) >= rank
    nt = (((1,), (1,)), ((), ()))

    r = rate(arrivals)
    hidden = jnp.zeros((token_count, 2 * rank), F32)
    for start, size in chunks:
        normed = (arrivals[:, start:start + size].astype(F32) * r).astype(BF16)
        hidden += jnp.dot(normed, weights[start:start + size, :], preferred_element_type=F32)
    hidden = hidden * features ** (-0.5)
    active = hidden / (1.0 + jnp.exp(-hidden))
    active = jnp.where(right, pltpu.roll(active, rank, 1), 0.0).astype(BF16)
    for start, size in chunks:
        branch = lax.dot_general(active, weights[start:start + size, :], nt, preferred_element_type=F32)
        y = arrivals[:, start:start + size].astype(F32) + branch * rank ** (-0.5)
        made[0, :, start:start + size] = y.astype(BF16)
    pl.semaphore_wait(barrier, greeted)
    spread(0)

    r = rate(kept)
    both = jnp.zeros((2 * token_count, 2 * rank), F32)
    for start, size in chunks:
        normed = (kept[:, start:start + size].astype(F32) * r).astype(BF16)
        stacked[:token_count, start:start + size] = normed
        stacked[token_count:, start:start + size] = returned[:, start:start + size]
        both += jnp.dot(stacked[:, start:start + size], weights[start:start + size, :], preferred_element_type=F32)
    hidden = both[:token_count] * features ** (-0.5)
    grad_active = pltpu.roll(both[token_count:], rank, 1) * rank ** (-0.5)
    logistic = 1.0 / (1.0 + jnp.exp(-hidden))
    active = jnp.where(right, pltpu.roll(hidden * logistic, rank, 1), 0.0).astype(BF16)
    grad_hidden = grad_active * logistic * (1.0 + hidden * (1.0 - logistic))
    grad_hidden = jnp.where(right, 0.0, grad_hidden).astype(BF16)
    mixed = jnp.zeros((token_count, 128), F32)
    for start, size in chunks:
        g = lax.dot_general(grad_hidden, weights[start:start + size, :], nt, preferred_element_type=F32)
        g = g * features ** (-0.5)
        grad_normed[:, start:start + size] = g
        g = g * kept[:, start:start + size].astype(F32)
        for c in range(0, size, 128):
            mixed += g[:, c:c + 128]
    mixed = jnp.sum(mixed, axis=1, keepdims=True) * (1.0 / features)
    pull = r * r * r * mixed
    for start, size in chunks:
        dx = (
            returned[:, start:start + size].astype(F32)
            + r * grad_normed[:, start:start + size]
            - kept[:, start:start + size].astype(F32) * pull
        )
        made[1, :, start:start + size] = dx.astype(BF16)
    spread(1)

    factors = jnp.concatenate([grad_hidden, active], axis=0)
    scale = jnp.where(
        lax.broadcasted_iota(jnp.int32, (1, 2 * rank), 1) >= rank, rank ** (-0.5), features ** (-0.5)
    )
    step = math.lcm(shard, 128)
    for start in range(0, features, step):
        g = lax.dot_general(
            stacked[:, start:start + step], factors, (((0,), (0,)), ((), ())), preferred_element_type=F32
        ) * scale
        for i in range(step // shard):
            j = start // shard + i
            z, q = divmod(j, inner)
            rows = g[i * shard:(i + 1) * shard]
            grad_wide[q, z * shard:(z + 1) * shard] = rows
            grad_sent[q, z * shard:(z + 1) * shard] = rows.astype(BF16)

    def send_plane(k, carry):
        q = lax.rem(spot + k, inner)
        pltpu.make_async_remote_copy(
            grad_sent.at[q], grad_landed.at[spot], sems.at[8], sems.at[9],
            device_id=(sec, plane * inner + q), device_id_type=MESH,
        ).start()
        return carry
    lax.fori_loop(1, inner, send_plane, 0)

    collect(0, source_on, onto, handed)

    less = pl.ds(0, inner - 1)
    pltpu.make_async_copy(grad_sent.at[less], grad_landed.at[less], sems.at[9]).wait()
    for z in range(outer):
        rows = pl.ds(z * shard, shard)
        total = grad_wide[spot, rows]
        for k in range(1, inner):
            total += grad_landed[lax.rem(spot + k, inner), rows].astype(F32)
        part_wide[z] = total
        part_sent[z] = total.astype(BF16)

    def send_line(k, carry):
        z = lax.rem(plane + k, outer)
        pltpu.make_async_remote_copy(
            part_sent.at[z], part_landed.at[plane], sems.at[10], sems.at[11],
            device_id=(sec, z * inner + spot), device_id_type=MESH,
        ).start()
        return carry
    lax.fori_loop(1, outer, send_line, 0)

    collect(1, source_back, back, passed)

    few = pl.ds(0, outer - 1)
    pltpu.make_async_copy(part_sent.at[few], part_landed.at[few], sems.at[11]).wait()
    grad = part_wide[plane]
    for k in range(1, outer):
        grad += part_landed[lax.rem(plane + k, outer)].astype(F32)
    first = beta_first * moment[...] + (1.0 - beta_first) * grad
    other = beta_second * second[...] + (1.0 - beta_second) * grad * grad
    update = first / first_correction / (jnp.sqrt(other / second_correction) + adam_eps)
    new_moment[...] = first
    new_second[...] = other
    new_master[...] = master[...] - learn_rate * (update + weight_decay * master[...])

    most = pl.ds(0, peers - 1)
    for t, result in ((0, handed), (1, passed)):
        pltpu.make_async_copy(landings[t].at[most], landings[t].at[most], sems.at[t]).wait()
        pltpu.make_async_copy(outgoing.at[t], outgoing.at[t], sems.at[4 + t]).wait()
        pltpu.make_async_copy(result, result, sems.at[6 + t]).wait()
    pltpu.make_async_copy(grad_sent.at[less], grad_sent.at[less], sems.at[8]).wait()
    pltpu.make_async_copy(part_sent.at[few], part_sent.at[few], sems.at[10]).wait()


def plane_size(peers):
    size = 1
    while size * size < peers:
        size *= 2
    return size


def shards(sections, arrivals, kept, returned, onward, backward_route, replicas, master, moment, second):
    peers = lax.axis_size("peer")
    token_count, features = arrivals.shape[2:]
    lanes = replicas.shape[3]
    shard = master.shape[1]
    inner = plane_size(peers)
    outer = peers // inner
    col_groups = peers // (token_count // ROWS)
    width = -(-features // (col_groups * 128)) * 128
    padded = width * col_groups
    vmem = pl.BlockSpec(memory_space=pltpu.VMEM)
    smem = pl.BlockSpec(memory_space=pltpu.SMEM)
    rows = jax.ShapeDtypeStruct((shard, lanes), F32)
    block = jax.ShapeDtypeStruct((token_count, padded), BF16)
    handed, passed, new_master, new_moment, new_second = pl.pallas_call(
        functools.partial(kernel, sections, peers, inner, width),
        out_shape=(block, block, rows, rows, rows),
        in_specs=[smem] * 2 + [vmem] * 7,
        out_specs=(vmem,) * 5,
        scratch_shapes=[
            pltpu.VMEM((2, token_count, padded), BF16),
            pltpu.VMEM((peers, ROWS, width), BF16),
            pltpu.VMEM((peers, ROWS, width), BF16),
            pltpu.VMEM((2, peers, ROWS, width), BF16),
            pltpu.VMEM((token_count, features), F32),
            pltpu.VMEM((2 * token_count, features), BF16),
            pltpu.VMEM((inner, outer * shard, lanes), F32),
            pltpu.VMEM((inner, outer * shard, lanes), BF16),
            pltpu.VMEM((inner, outer * shard, lanes), BF16),
            pltpu.VMEM((outer, shard, lanes), F32),
            pltpu.VMEM((outer, shard, lanes), BF16),
            pltpu.VMEM((outer, shard, lanes), BF16),
            pltpu.SemaphoreType.DMA((12,)),
        ],
        compiler_params=pltpu.CompilerParams(
            collective_id=0, has_side_effects=True, vmem_limit_bytes=48 * 1024 * 1024
        ),
        name="routed_step",
    )(
        inverse_order(onward[0]), inverse_order(backward_route[0]),
        arrivals[0, 0], kept[0, 0], returned[0, 0], replicas[0, 0], master[0], moment[0], second[0],
    )
    return (
        handed[None, None, :, :features], passed[None, None, :, :features],
        new_master[None], new_moment[None], new_second[None],
    )


def solution(mesh):
    whole = P("section", "peer", None, None)
    rows = P("section", "peer", None)
    table = P("section", None)
    return jax.shard_map(
        functools.partial(shards, mesh.shape["section"]),
        mesh=mesh,
        in_specs=(whole, whole, whole, table, table, whole, rows, rows, rows),
        out_specs=(whole, whole, rows, rows, rows),
        check_vma=False,
    )
```

time: 201 us -> 83.1 us (0.41); the launches traced: 198 us -> 82.8 us
  waiting for transfers between devices: 132 us -> 0 us
  Pallas kernels: 0 us -> 70.4 us
  starting transfers between devices: 27.8 us -> 0 us
  between operations: 14.2 us -> 0.66 us
  other arithmetic: 7.48 us -> 0.76 us
  matrix products: 5.05 us -> 0 us
    pallas_call x0 -> x1, Pallas kernels: none -> 70.4 us  [shards(): pl.pallas_call(functools.partial(kernel, sections, peers, inner, width),...]
    all_to_all x4 -> x0, waiting for transfers between devices: 69.3 us -> none  [the longest x1 26.1 us: spread_pair(): lax.all_to_all(onward_rows, 'peer', split_axis=0, concat_axis=0, tiled=True)]
    psum x1 -> x0, waiting for transfers between devices: 62.3 us -> none  [shards(): summed = lax.psum(gradient, 'peer')]
    all_to_all x4 -> x0, starting transfers between devices: 24.2 us -> none  [the longest x1 6.83 us: spread_pair(): lax.all_to_all(onward_rows, 'peer', split_axis=0, concat_axis=0, tiled=True)]
    unnamed x24 -> x19, local copies, waits for them, and re-layouts: 4.36 us -> 11 us
    reshape x4 -> x0, local copies, waits for them, and re-layouts: 5.37 us -> none  [the longest x1 2.23 us: shards(): handed = handed.reshape(1, 1, token_count, features)]
    dot_general x6 -> x0, matrix products: 5.05 us -> none  [the longest x1 2.03 us: backward_layer(): jnp.dot(normed, weights[:, :inner_rank], preferred_element_type=jnp.float32)]
    ppermute x2 -> x0, starting transfers between devices: 3.58 us -> none  [shifted(): return lax.ppermute(block, axis, route)]
  transfers between devices with their start and end apart: 7 -> 0, of which waited for: 5 -> 0; matrix products, arithmetic and copies ran while one was open for 7% -> 0% of each run, Pallas kernels for 0% -> 0%
where the time goes in v1:
time: 83.1 us; the launch traced here: 82.8 us
  Pallas kernels  70.4 us (85%)
  local copies, waits for them, and re-layouts  11 us (13%)
    pallas_call x1, Pallas kernels, shards(): pl.pallas_call(functools.partial(kernel, sections, peers, inner, width),...  70.4 us
    unnamed x19, local copies, waits for them, and re-layouts  11 us

profile of v1, /device:TPU:15, one launch (start us, length us, event | category | flops | bytes accessed | tf_op | source)
XLA Modules:
  0.0 82.8 jit_solution(10153809146412989736)
XLA Ops:
  0.6 0.8 select_reduce_fusion
  1.4 0.0 copy-start
  1.4 1.3 %copy-done = bf16[1,1,5120,128]{3,2,1,0:T(8,128)(2,1)S(1)} copy-done((bf16[1,1,5120,128]{3,2,1,0:T(8,128)(2,1)S(1)}, bf16[1,1,5120,128]{3,2,1,0:T(8,128)(2,1)}, u32[]{:S(2)}) %copy-start) | copy-done | bytes 1310744
  2.7 0.0 copy-start.1
  2.7 1.1 %copy-done.1 = bf16[1,1,64,5120]{3,2,1,0:T(8,128)(2,1)S(1)} copy-done((bf16[1,1,64,5120]{3,2,1,0:T(8,128)(2,1)S(1)}, bf16[1,1,64,5120]{3,2,1,0:T(8,128)(2,1)}, u32[]{:S(2)}) %copy-start.1) | copy-done | bytes 655384
  3.8 0.0 copy-start.2
  3.8 1.1 %copy-done.2 = bf16[1,1,64,5120]{3,2,1,0:T(8,128)(2,1)S(1)} copy-done((bf16[1,1,64,5120]{3,2,1,0:T(8,128)(2,1)S(1)}, bf16[1,1,64,5120]{3,2,1,0:T(8,128)(2,1)}, u32[]{:S(2)}) %copy-start.2) | copy-done | bytes 655384
  4.9 0.0 copy-start.3
  4.9 1.1 %copy-done.3 = bf16[1,1,64,5120]{3,2,1,0:T(8,128)(2,1)S(1)} copy-done((bf16[1,1,64,5120]{3,2,1,0:T(8,128)(2,1)S(1)}, bf16[1,1,64,5120]{3,2,1,0:T(8,128)(2,1)}, u32[]{:S(2)}) %copy-start.3) | copy-done | bytes 655384
  6.0 0.0 copy-start.4
  6.0 0.9 %copy-done.4 = f32[1,320,128]{2,1,0:T(8,128)S(1)} copy-done((f32[1,320,128]{2,1,0:T(8,128)S(1)}, f32[1,320,128]{2,1,0:T(8,128)}, u32[]{:S(2)}) %copy-start.4) | copy-done | bytes 163864
  6.9 0.0 copy-start.5
  6.9 0.9 %copy-done.5 = f32[1,320,128]{2,1,0:T(8,128)S(1)} copy-done((f32[1,320,128]{2,1,0:T(8,128)S(1)}, f32[1,320,128]{2,1,0:T(8,128)}, u32[]{:S(2)}) %copy-start.5) | copy-done | bytes 163864
  7.8 0.0 copy-start.6
  7.8 0.9 %copy-done.6 = f32[1,320,128]{2,1,0:T(8,128)S(1)} copy-done((f32[1,320,128]{2,1,0:T(8,128)S(1)}, f32[1,320,128]{2,1,0:T(8,128)}, u32[]{:S(2)}) %copy-start.6) | copy-done | bytes 163864
  8.7 70.4 %routed_step.1 = (bf16[64,5120]{1,0:T(8,128)(2,1)S(1)}, bf16[64,5120]{1,0:T(8,128)(2,1)S(1)}, f32[320,128]{1,0:T(8,128)S(1)}, f32[320,128]{1,0:T(8,128)S(1)}, f32[320,128]{1,0:T(8,128)S(1)}) custom-call(s32[16]{0:T(128)S(1)} %get-tuple-element.16.source_on, s32[16]{0:T(128)S(1)} %get-tuple-element.15.source_back, bf16[64,5120]{1,0:T(8,128)(2,1)S(1)} %bitcast.17, ...), custom_call_target="tpu_custom_call" | custom-call | tf_op jit(solution)/shard_map/routed_step/pallas_call | solution.py:255
  79.1 0.8 %copy.19 = bf16[1,1,64,5120]{3,2,1,0:T(8,128)(2,1)} copy(bf16[1,1,64,5120]{3,2,1,0:T(8,128)(2,1)S(1)} %bitcast.16) | data formatting | bytes 1310720
  79.9 0.8 %copy.20 = bf16[1,1,64,5120]{3,2,1,0:T(8,128)(2,1)} copy(bf16[1,1,64,5120]{3,2,1,0:T(8,128)(2,1)S(1)} %bitcast.15) | data formatting | bytes 1310720
  80.8 0.7 copy.21
  81.4 0.7 copy.22
  82.1 0.7 copy.23
Async XLA Ops:
  1.4 1.3 %copy-start = (bf16[1,1,5120,128]{3,2,1,0:T(8,128)(2,1)S(1)}, bf16[1,1,5120,128]{3,2,1,0:T(8,128)(2,1)}, u32[]{:S(2)}) copy-start(bf16[1,1,5120,128]{3,2,1,0:T(8,128)(2,1)} %param.14) | copy-start | bytes 3932164
  2.7 1.1 %copy-start.1 = (bf16[1,1,64,5120]{3,2,1,0:T(8,128)(2,1)S(1)}, bf16[1,1,64,5120]{3,2,1,0:T(8,128)(2,1)}, u32[]{:S(2)}) copy-start(bf16[1,1,64,5120]{3,2,1,0:T(8,128)(2,1)} %param.9) | copy-start | bytes 1966084
  3.8 1.1 %copy-start.2 = (bf16[1,1,64,5120]{3,2,1,0:T(8,128)(2,1)S(1)}, bf16[1,1,64,5120]{3,2,1,0:T(8,128)(2,1)}, u32[]{:S(2)}) copy-start(bf16[1,1,64,5120]{3,2,1,0:T(8,128)(2,1)} %param.10) | copy-start | bytes 1966084
  4.9 1.1 %copy-start.3 = (bf16[1,1,64,5120]{3,2,1,0:T(8,128)(2,1)S(1)}, bf16[1,1,64,5120]{3,2,1,0:T(8,128)(2,1)}, u32[]{:S(2)}) copy-start(bf16[1,1,64,5120]{3,2,1,0:T(8,128)(2,1)} %param.11) | copy-start | bytes 1966084
  6.0 0.9 %copy-start.4 = (f32[1,320,128]{2,1,0:T(8,128)S(1)}, f32[1,320,128]{2,1,0:T(8,128)}, u32[]{:S(2)}) copy-start(f32[1,320,128]{2,1,0:T(8,128)} %param.15) | copy-start | bytes 491524
  6.9 0.9 %copy-start.5 = (f32[1,320,128]{2,1,0:T(8,128)S(1)}, f32[1,320,128]{2,1,0:T(8,128)}, u32[]{:S(2)}) copy-start(f32[1,320,128]{2,1,0:T(8,128)} %param.16) | copy-start | bytes 491524
  7.8 0.9 %copy-start.6 = (f32[1,320,128]{2,1,0:T(8,128)S(1)}, f32[1,320,128]{2,1,0:T(8,128)}, u32[]{:S(2)}) copy-start(f32[1,320,128]{2,1,0:T(8,128)} %param.17) | copy-start | bytes 491524

commit v2 on v1

--- a/solution.py
+++ b/solution.py
@@ -22,12 +22,6 @@
 F32, BF16 = jnp.float32, jnp.bfloat16
 
 
-def inverse_order(targets):
-    positions = jnp.arange(targets.shape[0], dtype=jnp.int32)
-    matches = (targets[:, None] == positions[None, :]).astype(jnp.int32)
-    return jnp.sum(matches * positions[:, None], axis=0)
-
-
 def column_chunks(width, parts):
     step = width // parts
     return [(i * step, step) for i in range(parts)]
@@ -35,10 +29,21 @@
 
 def kernel(
     sections, peers, inner, width,
-    source_on, source_back, arrivals, kept, returned, weights, master, moment, second,
+    table_on, table_back, *refs,
+):
+    operands, refs = refs[:7], refs[7:]
+    results, refs = refs[:5], refs[5:]
+    staged, refs = refs[:7], refs[7:]
+    step(sections, peers, inner, width, table_on, table_back, operands, *staged, *results, *refs)
+
+
+def step(
+    sections, peers, inner, width, table_on, table_back, operands,
+    arrivals, kept, returned, weights, master, moment, second,
     handed, passed, new_master, new_moment, new_second,
     made, landed_on, landed_back, outgoing, grad_normed, stacked, grad_wide, grad_sent, grad_landed,
-    part_wide, part_sent, part_landed, sems,
+    part_wide, part_sent, part_landed, far_wide, far_sent, far_landed,
+    first_out, second_out, master_out, source_on, source_back, load_sems, sems,
 ):
     token_count, features = arrivals.shape
     rank = weights.shape[1] // 2
@@ -50,6 +55,14 @@
     onto = lax.rem(sec + 1, sections)
     back = lax.rem(sec + sections - 1, sections)
 
+    loads = [
+        pltpu.make_async_copy(operand, here, load_sems.at[i])
+        for i, (operand, here) in enumerate(
+            zip(operands, (arrivals, kept, returned, weights, master, moment, second))
+        )
+    ]
+    for i in (0, 3, 1, 2, 4, 5, 6):
+        loads[i].start()
     landings = (landed_on, landed_back)
     barrier = pltpu.get_barrier_semaphore()
 
@@ -99,6 +112,15 @@
             return carry
         lax.fori_loop(0, peers, one, 0)
 
+    def invert(table, order):
+        def one(d, carry):
+            found = jnp.int32(0)
+            for p in range(1, peers):
+                found = jnp.where(table[p] == d, p, found)
+            order[d] = found
+            return carry
+        lax.fori_loop(0, peers, one, 0)
+
     chunks = column_chunks(features, 4)
     if made.shape[2] > features:
         made[:, :, features:] = jnp.zeros((2, token_count, made.shape[2] - features), BF16)
@@ -115,7 +137,9 @@
     right = lax.broadcasted_iota(jnp.int32, (token_count, 2 * rank), 1) >= rank
     nt = (((1,), (1,)), ((), ()))
 
+    loads[0].wait()
     r = rate(arrivals)
+    loads[3].wait()
     hidden = jnp.zeros((token_count, 2 * rank), F32)
     for start, size in chunks:
         normed = (arrivals[:, start:start + size].astype(F32) * r).astype(BF16)
@@ -130,6 +154,8 @@
     pl.semaphore_wait(barrier, greeted)
     spread(0)
 
+    loads[1].wait()
+    loads[2].wait()
     r = rate(kept)
     both = jnp.zeros((2 * token_count, 2 * rank), F32)
     for start, size in chunks:
@@ -187,8 +213,11 @@
         return carry
     lax.fori_loop(1, inner, send_plane, 0)
 
+    invert(table_on, source_on)
+    invert(table_back, source_back)
     collect(0, source_on, onto, handed)
 
+    parity, pair = lax.rem(plane, 2), plane // 2
     less = pl.ds(0, inner - 1)
     pltpu.make_async_copy(grad_sent.at[less], grad_landed.at[less], sems.at[9]).wait()
     for z in range(outer):
@@ -196,31 +225,52 @@
         total = grad_wide[spot, rows]
         for k in range(1, inner):
             total += grad_landed[lax.rem(spot + k, inner), rows].astype(F32)
-        part_wide[z] = total
-        part_sent[z] = total.astype(BF16)
-
-    def send_line(k, carry):
-        z = lax.rem(plane + k, outer)
+        part_wide[z % 2, z // 2] = total
+        part_sent[z % 2, z // 2] = total.astype(BF16)
+    pair_copy = pltpu.make_async_remote_copy(
+        part_sent.at[1 - parity], part_landed, sems.at[10], sems.at[11],
+        device_id=(sec, (plane + 1 - 2 * parity) * inner + spot), device_id_type=MESH,
+    )
+    pair_copy.start()
+
+    collect(1, source_back, back, passed)
+
+    pair_copy.wait_recv()
+    pairs = outer // 2
+    for h in range(pairs):
+        total = part_wide[parity, h] + part_landed[h].astype(F32)
+        far_wide[h] = total
+        far_sent[h] = total.astype(BF16)
+
+    def send_far(k, carry):
+        h = lax.rem(pair + k, pairs)
         pltpu.make_async_remote_copy(
-            part_sent.at[z], part_landed.at[plane], sems.at[10], sems.at[11],
-            device_id=(sec, z * inner + spot), device_id_type=MESH,
+            far_sent.at[h], far_landed.at[pair], sems.at[12], sems.at[13],
+            device_id=(sec, (2 * h + parity) * inner + spot), device_id_type=MESH,
         ).start()
         return carry
-    lax.fori_loop(1, outer, send_line, 0)
-
-    collect(1, source_back, back, passed)
-
-    few = pl.ds(0, outer - 1)
-    pltpu.make_async_copy(part_sent.at[few], part_landed.at[few], sems.at[11]).wait()
-    grad = part_wide[plane]
-    for k in range(1, outer):
-        grad += part_landed[lax.rem(plane + k, outer)].astype(F32)
+    lax.fori_loop(1, pairs, send_far, 0)
+
+    few = pl.ds(0, pairs - 1)
+    pltpu.make_async_copy(far_sent.at[few], far_landed.at[few], sems.at[13]).wait()
+    grad = far_wide[pair]
+    for k in range(1, pairs):
+        grad += far_landed[lax.rem(pair + k, pairs)].astype(F32)
+    for i in (4, 5, 6):
+        loads[i].wait()
     first = beta_first * moment[...] + (1.0 - beta_first) * grad
     other = beta_second * second[...] + (1.0 - beta_second) * grad * grad
     update = first / first_correction / (jnp.sqrt(other / second_correction) + adam_eps)
-    new_moment[...] = first
-    new_second[...] = other
-    new_master[...] = master[...] - learn_rate * (update + weight_decay * master[...])
+    first_out[...] = first
+    second_out[...] = other
+    master_out[...] = master[...] - learn_rate * (update + weight_decay * master[...])
+    stores = [
+        pltpu.make_async_copy(first_out, new_moment, load_sems.at[7]),
+        pltpu.make_async_copy(second_out, new_second, load_sems.at[8]),
+        pltpu.make_async_copy(master_out, new_master, load_sems.at[9]),
+    ]
+    for copy in stores:
+        copy.start()
 
     most = pl.ds(0, peers - 1)
     for t, result in ((0, handed), (1, passed)):
@@ -228,7 +278,24 @@
         pltpu.make_async_copy(outgoing.at[t], outgoing.at[t], sems.at[4 + t]).wait()
         pltpu.make_async_copy(result, result, sems.at[6 + t]).wait()
     pltpu.make_async_copy(grad_sent.at[less], grad_sent.at[less], sems.at[8]).wait()
-    pltpu.make_async_copy(part_sent.at[few], part_sent.at[few], sems.at[10]).wait()
+    pair_copy.wait_send()
+    pltpu.make_async_copy(far_sent.at[few], far_sent.at[few], sems.at[12]).wait()
+    for copy in stores:
+        copy.wait()
+
+
+def deliver(*refs):
+    sources, results, staged, arrived, left = refs[:5], refs[5:10], refs[10:15], refs[15], refs[16]
+    loads = [pltpu.make_async_copy(sources[i], staged[i], arrived.at[i]) for i in range(5)]
+    stores = [pltpu.make_async_copy(staged[i], results[i], left.at[i]) for i in range(5)]
+    order = (2, 3, 4, 0, 1)
+    for i in order:
+        loads[i].start()
+    for i in order:
+        loads[i].wait()
+        stores[i].start()
+    for i in order:
+        stores[i].wait()
 
 
 def plane_size(peers):
@@ -248,16 +315,19 @@
     col_groups = peers // (token_count // ROWS)
     width = -(-features // (col_groups * 128)) * 128
     padded = width * col_groups
-    vmem = pl.BlockSpec(memory_space=pltpu.VMEM)
+    hbm = pl.BlockSpec(memory_space=pltpu.HBM)
     smem = pl.BlockSpec(memory_space=pltpu.SMEM)
     rows = jax.ShapeDtypeStruct((shard, lanes), F32)
     block = jax.ShapeDtypeStruct((token_count, padded), BF16)
-    handed, passed, new_master, new_moment, new_second = pl.pallas_call(
+    operands = (
+        arrivals[0, 0], kept[0, 0], returned[0, 0], replicas[0, 0], master[0], moment[0], second[0],
+    )
+    results = pl.pallas_call(
         functools.partial(kernel, sections, peers, inner, width),
         out_shape=(block, block, rows, rows, rows),
-        in_specs=[smem] * 2 + [vmem] * 7,
-        out_specs=(vmem,) * 5,
-        scratch_shapes=[
+        in_specs=[smem] * 2 + [hbm] * 7,
+        out_specs=(hbm,) * 5,
+        scratch_shapes=[pltpu.VMEM(a.shape, a.dtype) for a in operands] + [
             pltpu.VMEM((2, token_count, padded), BF16),
             pltpu.VMEM((peers, ROWS, width), BF16),
             pltpu.VMEM((peers, ROWS, width), BF16),
@@ -267,19 +337,37 @@
             pltpu.VMEM((inner, outer * shard, lanes), F32),
             pltpu.VMEM((inner, outer * shard, lanes), BF16),
             pltpu.VMEM((inner, outer * shard, lanes), BF16),
-            pltpu.VMEM((outer, shard, lanes), F32),
-            pltpu.VMEM((outer, shard, lanes), BF16),
-            pltpu.VMEM((outer, shard, lanes), BF16),
-            pltpu.SemaphoreType.DMA((12,)),
+            pltpu.VMEM((2, outer // 2, shard, lanes), F32),
+            pltpu.VMEM((2, outer // 2, shard, lanes), BF16),
+            pltpu.VMEM((outer // 2, shard, lanes), BF16),
+            pltpu.VMEM((outer // 2, shard, lanes), F32),
+            pltpu.VMEM((outer // 2, shard, lanes), BF16),
+            pltpu.VMEM((outer // 2, shard, lanes), BF16),
+            pltpu.VMEM((shard, lanes), F32),
+            pltpu.VMEM((shard, lanes), F32),
+            pltpu.VMEM((shard, lanes), F32),
+            pltpu.SMEM((peers,), jnp.int32),
+            pltpu.SMEM((peers,), jnp.int32),
+            pltpu.SemaphoreType.DMA((10,)),
+            pltpu.SemaphoreType.DMA((14,)),
         ],
         compiler_params=pltpu.CompilerParams(
-            collective_id=0, has_side_effects=True, vmem_limit_bytes=48 * 1024 * 1024
+            collective_id=0, has_side_effects=True, vmem_limit_bytes=64 * 1024 * 1024 - 65536
         ),
         name="routed_step",
     )(
-        inverse_order(onward[0]), inverse_order(backward_route[0]),
-        arrivals[0, 0], kept[0, 0], returned[0, 0], replicas[0, 0], master[0], moment[0], second[0],
-    )
+        onward[0], backward_route[0], *operands
+    )
+    handed, passed, new_master, new_moment, new_second = pl.pallas_call(
+        deliver,
+        out_shape=(block, block, rows, rows, rows),
+        in_specs=[hbm] * 5,
+        out_specs=(hbm,) * 5,
+        scratch_shapes=[pltpu.VMEM(a.shape, a.dtype) for a in (block, block, rows, rows, rows)]
+        + [pltpu.SemaphoreType.DMA((5,)), pltpu.SemaphoreType.DMA((5,))],
+        compiler_params=pltpu.CompilerParams(vmem_limit_bytes=64 * 1024 * 1024 - 65536),
+        name="deliver",
+    )(*results)
     return (
         handed[None, None, :, :features], passed[None, None, :, :features],
         new_master[None], new_moment[None], new_second[None],

time: 83.1 us -> 73.7 us (0.89)
  the two profiles are of different devices: /device:TPU:15 before, /device:TPU:0 now
where the time goes in v2:
time: 73.7 us; the launch traced here: 73.6 us
  Pallas kernels  72.9 us (99%)
    pallas_call x1, Pallas kernels, shards(): pl.pallas_call(functools.partial(kernel, sections, peers, inner, width),...  70.5 us
    pallas_call x1, Pallas kernels, shards(): pl.pallas_call(deliver, out_shape=(block, block, rows, rows, rows), in_sp...  2.48 us

profile of v2, /device:TPU:0, one launch (start us, length us, event | category | flops | bytes accessed | tf_op | source)
XLA Modules:
  0.0 73.6 jit_solution(3438909255050085306)
XLA Ops:
  0.6 70.5 %routed_step.1 = (bf16[64,5120]{1,0:T(8,128)(2,1)}, bf16[64,5120]{1,0:T(8,128)(2,1)}, f32[320,128]{1,0:T(8,128)}, f32[320,128]{1,0:T(8,128)}, f32[320,128]{1,0:T(8,128)}) custom-call(s32[16]{0:T(128)} %bitcast.21, s32[16]{0:T(128)} %bitcast.22, bf16[64,5120]{1,0:T(8,128)(2,1)} %bitcast.15, bf16[64,5120]{1,0:T(8,128)(2,1)} %bitcast.16, ...), custom_call_target="tpu_custom_call" | custom-call | tf_op jit(solution)/shard_map/routed_step/pallas_call | solution.py:325
  71.1 2.5 %deliver.1 = (bf16[64,5120]{1,0:T(8,128)(2,1)}, bf16[64,5120]{1,0:T(8,128)(2,1)}, f32[320,128]{1,0:T(8,128)}, f32[320,128]{1,0:T(8,128)}, f32[320,128]{1,0:T(8,128)}) custom-call(bf16[64,5120]{1,0:T(8,128)(2,1)} %get-tuple-element.15.refs_0_, bf16[64,5120]{1,0:T(8,128)(2,1)} %get-tuple-element.16.refs_1_, f32[320,128]{1,0:T(8,128)} %get-tuple-element.17.refs_2_, ...), custom_call_target="tpu_custom_call" | custom-call | tf_op jit(solution)/shard_map/deliver/pallas_call | solution.py:361

commit v3 on v2

--- a/solution.py
+++ b/solution.py
@@ -147,12 +147,36 @@
     hidden = hidden * features ** (-0.5)
     active = hidden / (1.0 + jnp.exp(-hidden))
     active = jnp.where(right, pltpu.roll(active, rank, 1), 0.0).astype(BF16)
-    for start, size in chunks:
-        branch = lax.dot_general(active, weights[start:start + size, :], nt, preferred_element_type=F32)
-        y = arrivals[:, start:start + size].astype(F32) + branch * rank ** (-0.5)
-        made[0, :, start:start + size] = y.astype(BF16)
-    pl.semaphore_wait(barrier, greeted)
-    spread(0)
+    pieced = width * col_groups == features and col_groups <= 4
+    if not pieced:
+        for start, size in chunks:
+            branch = lax.dot_general(active, weights[start:start + size, :], nt, preferred_element_type=F32)
+            y = arrivals[:, start:start + size].astype(F32) + branch * rank ** (-0.5)
+            made[0, :, start:start + size] = y.astype(BF16)
+        pl.semaphore_wait(barrier, greeted)
+        spread(0)
+    else:
+        row_groups = peers // col_groups
+        for i in range(col_groups):
+            group = lax.rem(me + i, col_groups)
+            part = pl.ds(pl.multiple_of(group * width, 128), width)
+            branch = lax.dot_general(active, weights[part, :], nt, preferred_element_type=F32)
+            y = arrivals[:, part].astype(F32) + branch * rank ** (-0.5)
+            made[0, :, part] = y.astype(BF16)
+            if i == 0:
+                pl.semaphore_wait(barrier, greeted)
+
+            def one(k, carry):
+                j = lax.rem(me // col_groups + k, row_groups) * col_groups + group
+                rows, cols = piece(j)
+                pltpu.make_async_remote_copy(
+                    made.at[0, rows, cols], landed_on.at[me], sems.at[0], sems.at[2],
+                    device_id=(sec, j), device_id_type=MESH,
+                ).start()
+                return carry
+            lax.fori_loop(1 if i == 0 else 0, row_groups, one, 0)
+        rows, cols = piece(me)
+        pltpu.make_async_copy(made.at[0, rows, cols], landed_on.at[me], sems.at[2]).start()
 
     loads[1].wait()
     loads[2].wait()
@@ -233,8 +257,6 @@
     )
     pair_copy.start()
 
-    collect(1, source_back, back, passed)
-
     pair_copy.wait_recv()
     pairs = outer // 2
     for h in range(pairs):
@@ -250,6 +272,8 @@
         ).start()
         return carry
     lax.fori_loop(1, pairs, send_far, 0)
+
+    collect(1, source_back, back, passed)
 
     few = pl.ds(0, pairs - 1)
     pltpu.make_async_copy(far_sent.at[few], far_landed.at[few], sems.at[13]).wait()

time: 73.7 us -> 70.6 us (0.958)
  the two profiles are of different devices: /device:TPU:0 before, /device:TPU:15 now
where the time goes in v3:
time: 70.6 us; the launch traced here: 70.5 us
  Pallas kernels  69.8 us (99%)
    pallas_call x1, Pallas kernels, shards(): pl.pallas_call(functools.partial(kernel, sections, peers, inner, width),...  67.3 us
    pallas_call x1, Pallas kernels, shards(): pl.pallas_call(deliver, out_shape=(block, block, rows, rows, rows), in_sp...  2.48 us

profile of v3, /device:TPU:15, one launch (start us, length us, event | category | flops | bytes accessed | tf_op | source)
XLA Modules:
  0.0 70.5 jit_solution(1028576735177254182)
XLA Ops:
  0.6 67.3 %routed_step.1 = (bf16[64,5120]{1,0:T(8,128)(2,1)}, bf16[64,5120]{1,0:T(8,128)(2,1)}, f32[320,128]{1,0:T(8,128)}, f32[320,128]{1,0:T(8,128)}, f32[320,128]{1,0:T(8,128)}) custom-call(s32[16]{0:T(128)} %bitcast.21, s32[16]{0:T(128)} %bitcast.22, bf16[64,5120]{1,0:T(8,128)(2,1)} %bitcast.15, bf16[64,5120]{1,0:T(8,128)(2,1)} %bitcast.16, ...), custom_call_target="tpu_custom_call" | custom-call | tf_op jit(solution)/shard_map/routed_step/pallas_call | solution.py:349
  68.0 2.5 %deliver.1 = (bf16[64,5120]{1,0:T(8,128)(2,1)}, bf16[64,5120]{1,0:T(8,128)(2,1)}, f32[320,128]{1,0:T(8,128)}, f32[320,128]{1,0:T(8,128)}, f32[320,128]{1,0:T(8,128)}) custom-call(bf16[64,5120]{1,0:T(8,128)(2,1)} %get-tuple-element.15.refs_0_, bf16[64,5120]{1,0:T(8,128)(2,1)} %get-tuple-element.16.refs_1_, f32[320,128]{1,0:T(8,128)} %get-tuple-element.17.refs_2_, ...), custom_call_target="tpu_custom_call" | custom-call | tf_op jit(solution)/shard_map/deliver/pallas_call | solution.py:385
